TPU v7x, 128 devices: a whole 4x4x4 slice. The times are simulated.
128 devices in a mesh: lb: 8 (over z_lo, x), rb: 16 (over z_hi, y, core).
Axes of the slice: x: 4, y: 4, z: 4 (z_hi: 2, z_lo: 2; z = z_hi * 2 + z_lo), core: 2. Of those that a mesh axis runs over, the one named last changes fastest.
Arguments:
- psi: bfloat16 [16384, 8192], P('lb', 'rb'), may hold values from -6 to 6
- left_env: bfloat16 [28, 16384, 128], P(None, 'lb'), may hold values from -0.5 to 0.5
- right_env: bfloat16 [28, 8192, 128], P(None, 'rb'), may hold values from -0.09375 to 0.09375
- left_src: int32 [28, 128], replicated, may hold values from 0 to 127, as said below
- right_dst: int32 [28, 64], replicated, may hold values from 0 to 63, as said below
Outputs:
- h_psi: bfloat16 [16384, 8192], P('lb', 'rb')
Inputs may be any that keep to these rules, and one draw needn't show every extreme that they name: `left_src`: each entry differs from its block index i by at most 2, and that distance is reached. `right_dst`: each entry differs from its block index j by at most 2, and that distance is reached.
All inputs are finite; a program needn't handle non-finite values.
Results may differ from a plain program's by a relative error of at most 0.0049.
Values may be sent and summed in bfloat16 or wider, within the bound.
A program may use at most 128 MiB of HBM per device.

v0:
```python
import jax
import jax.numpy as jnp
from jax import lax
from jax.sharding import PartitionSpec as P

SPAN = 2


def padded(block, sides, width):
    for axis, dim in sides:
        count = lax.axis_size(axis)
        forward = [(i, i + 1) for i in range(count - 1)]
        backward = [(target, source) for source, target in forward]
        low = lax.ppermute(
            lax.slice_in_dim(block, block.shape[dim] - width, None, axis=dim), axis, forward
        )
        high = lax.ppermute(lax.slice_in_dim(block, 0, width, axis=dim), axis, backward)
        block = jnp.concatenate([low, block, high], axis=dim)
    return block


def from_behind(array, axis, by):
    size = lax.axis_size(axis)
    pairs = [(i, i + by) for i in range(size) if 0 <= i + by < size]
    return lax.ppermute(array, axis, pairs)


def on_device(psi, left_env, right_env, left_src, right_dst):
    local_rows, local_cols = psi.shape
    block_size = left_env.shape[2]
    terms_count = left_env.shape[0]
    left_count = local_rows // block_size
    right_count = local_cols // block_size
    left_start = lax.axis_index("lb") * left_count
    right_start = lax.axis_index("rb") * right_count
    source_index = lax.dynamic_slice_in_dim(left_src, left_start, left_count, 1) - (
        left_start - SPAN
    )
    left_blocks = left_env.reshape(terms_count, left_count, block_size, block_size)
    extended = padded(psi, (("lb", 0),), SPAN * block_size)
    target_index = (
        lax.dynamic_slice_in_dim(right_dst, right_start, right_count, 1) - right_start + SPAN
    )
    target_width = right_count + 2 * SPAN
    source_blocks = extended.reshape(-1, block_size, right_count * block_size)
    right_blocks = right_env.reshape(terms_count, right_count, block_size, block_size)

    def apply_term(term_index, totals):
        picked = jnp.take(source_blocks, source_index[term_index], axis=0)
        inner = jnp.einsum(
            "irc,icm->irm", left_blocks[term_index], picked, preferred_element_type=jnp.float32
        )
        inner = inner.astype(jnp.bfloat16).reshape(local_rows, right_count, block_size)
        contrib = jnp.einsum(
            "mjc,jce->mje", inner, right_blocks[term_index], preferred_element_type=jnp.float32
        )
        return totals.at[:, target_index[term_index]].add(contrib)

    totals = lax.fori_loop(
        0, terms_count, apply_term, jnp.zeros((local_rows, target_width, block_size), jnp.float32)
    )
    middle = totals[:, SPAN : SPAN + right_count]
    from_below = from_behind(totals[:, SPAN + right_count :], "rb", 1)
    from_above = from_behind(totals[:, :SPAN], "rb", -1)
    middle = middle.at[:, :SPAN].add(from_below)
    middle = middle.at[:, right_count - SPAN :].add(from_above)
    return middle.reshape(local_rows, local_cols).astype(jnp.bfloat16)


def solution(mesh):
    return jax.shard_map(
        on_device,
        mesh=mesh,
        in_specs=(P("lb", "rb"), P(None, "lb", None), P(None, "rb", None), P(), P()),
        out_specs=P("lb", "rb"),
        check_vma=False,
    )
```

profile of v0, /device:TPU:25, one launch (start us, length us, event | category | flops | bytes accessed | tf_op | source)
XLA Modules:
  0.0 639.4 jit_solution(17935302422268359045)
XLA Ops:
  20.1 576.1 %while.15 = (s32[]{:T(128)}, f32[2048,8,128]{2,0,1:T(8,128)}, s32[28,4]{1,0:T(8,128)S(1)}, bf16[28,4,128,128]{3,2,1,0:T(8,128)(2,1)}, bf16[28,16,128,128]{3,2,1,...) while((s32[]{:T(128)}, f32[2048,8,128]{2,0,1:T(8,128)}, ...), condition=%wide.region_2.3_spmd, body=%wide.region_0.2_spmd.sunk | while | flops 540017792 | bytes 32117248 | solution.py:59
  31.8 9.0 %scatter_fusion = f32[2048,8,128]{2,0,1:T(8,128)} fusion(f32[2048,8,128]{2,0,1:T(8,128)} %get-tuple-element.224, s32[4]{0:T(128)S(1)} %fusion.34, f32[4,2048,128]{2,1,0:T(8,128)} %fusion.37), kind=kCustom, calls=%fused_computation.1.clone.1 | custom fusion | flops 1048576 | bytes 12582928 | tf_op jit(solution)/shard_map/while/body/eval_jaxpr/scatter-add | solution.py:57
  72.8 8.9 %scatter_fusion = f32[2048,8,128]{2,0,1:T(8,128)} fusion(f32[2048,8,128]{2,0,1:T(8,128)} %get-tuple-element.224, s32[4]{0:T(128)S(1)} %fusion.34, f32[4,2048,128]{2,1,0:T(8,128)} %fusion.37), kind=kCustom, calls=%fused_computation.1.clone.1 | custom fusion | flops 1048576 | bytes 12582928 | tf_op jit(solution)/shard_map/while/body/eval_jaxpr/scatter-add | solution.py:57
  93.5 8.9 %scatter_fusion = f32[2048,8,128]{2,0,1:T(8,128)} fusion(f32[2048,8,128]{2,0,1:T(8,128)} %get-tuple-element.224, s32[4]{0:T(128)S(1)} %fusion.34, f32[4,2048,128]{2,1,0:T(8,128)} %fusion.37), kind=kCustom, calls=%fused_computation.1.clone.1 | custom fusion | flops 1048576 | bytes 12582928 | tf_op jit(solution)/shard_map/while/body/eval_jaxpr/scatter-add | solution.py:57
  114.2 8.7 %scatter_fusion = f32[2048,8,128]{2,0,1:T(8,128)} fusion(f32[2048,8,128]{2,0,1:T(8,128)} %get-tuple-element.224, s32[4]{0:T(128)S(1)} %fusion.34, f32[4,2048,128]{2,1,0:T(8,128)} %fusion.37), kind=kCustom, calls=%fused_computation.1.clone.1 | custom fusion | flops 1048576 | bytes 12582928 | tf_op jit(solution)/shard_map/while/body/eval_jaxpr/scatter-add | solution.py:57
  134.6 8.7 %scatter_fusion = f32[2048,8,128]{2,0,1:T(8,128)} fusion(f32[2048,8,128]{2,0,1:T(8,128)} %get-tuple-element.224, s32[4]{0:T(128)S(1)} %fusion.34, f32[4,2048,128]{2,1,0:T(8,128)} %fusion.37), kind=kCustom, calls=%fused_computation.1.clone.1 | custom fusion | flops 1048576 | bytes 12582928 | tf_op jit(solution)/shard_map/while/body/eval_jaxpr/scatter-add | solution.py:57
  155.0 8.9 %scatter_fusion = f32[2048,8,128]{2,0,1:T(8,128)} fusion(f32[2048,8,128]{2,0,1:T(8,128)} %get-tuple-element.224, s32[4]{0:T(128)S(1)} %fusion.34, f32[4,2048,128]{2,1,0:T(8,128)} %fusion.37), kind=kCustom, calls=%fused_computation.1.clone.1 | custom fusion | flops 1048576 | bytes 12582928 | tf_op jit(solution)/shard_map/while/body/eval_jaxpr/scatter-add | solution.py:57
  216.3 9.1 %scatter_fusion = f32[2048,8,128]{2,0,1:T(8,128)} fusion(f32[2048,8,128]{2,0,1:T(8,128)} %get-tuple-element.224, s32[4]{0:T(128)S(1)} %fusion.34, f32[4,2048,128]{2,1,0:T(8,128)} %fusion.37), kind=kCustom, calls=%fused_computation.1.clone.1 | custom fusion | flops 1048576 | bytes 12582928 | tf_op jit(solution)/shard_map/while/body/eval_jaxpr/scatter-add | solution.py:57
  237.1 8.9 %scatter_fusion = f32[2048,8,128]{2,0,1:T(8,128)} fusion(f32[2048,8,128]{2,0,1:T(8,128)} %get-tuple-element.224, s32[4]{0:T(128)S(1)} %fusion.34, f32[4,2048,128]{2,1,0:T(8,128)} %fusion.37), kind=kCustom, calls=%fused_computation.1.clone.1 | custom fusion | flops 1048576 | bytes 12582928 | tf_op jit(solution)/shard_map/while/body/eval_jaxpr/scatter-add | solution.py:57
  257.8 9.0 %scatter_fusion = f32[2048,8,128]{2,0,1:T(8,128)} fusion(f32[2048,8,128]{2,0,1:T(8,128)} %get-tuple-element.224, s32[4]{0:T(128)S(1)} %fusion.34, f32[4,2048,128]{2,1,0:T(8,128)} %fusion.37), kind=kCustom, calls=%fused_computation.1.clone.1 | custom fusion | flops 1048576 | bytes 12582928 | tf_op jit(solution)/shard_map/while/body/eval_jaxpr/scatter-add | solution.py:57
  278.5 9.0 %scatter_fusion = f32[2048,8,128]{2,0,1:T(8,128)} fusion(f32[2048,8,128]{2,0,1:T(8,128)} %get-tuple-element.224, s32[4]{0:T(128)S(1)} %fusion.34, f32[4,2048,128]{2,1,0:T(8,128)} %fusion.37), kind=kCustom, calls=%fused_computation.1.clone.1 | custom fusion | flops 1048576 | bytes 12582928 | tf_op jit(solution)/shard_map/while/body/eval_jaxpr/scatter-add | solution.py:57
  299.2 8.7 %scatter_fusion = f32[2048,8,128]{2,0,1:T(8,128)} fusion(f32[2048,8,128]{2,0,1:T(8,128)} %get-tuple-element.224, s32[4]{0:T(128)S(1)} %fusion.34, f32[4,2048,128]{2,1,0:T(8,128)} %fusion.37), kind=kCustom, calls=%fused_computation.1.clone.1 | custom fusion | flops 1048576 | bytes 12582928 | tf_op jit(solution)/shard_map/while/body/eval_jaxpr/scatter-add | solution.py:57
  319.6 9.0 %scatter_fusion = f32[2048,8,128]{2,0,1:T(8,128)} fusion(f32[2048,8,128]{2,0,1:T(8,128)} %get-tuple-element.224, s32[4]{0:T(128)S(1)} %fusion.34, f32[4,2048,128]{2,1,0:T(8,128)} %fusion.37), kind=kCustom, calls=%fused_computation.1.clone.1 | custom fusion | flops 1048576 | bytes 12582928 | tf_op jit(solution)/shard_map/while/body/eval_jaxpr/scatter-add | solution.py:57
  340.3 9.0 %scatter_fusion = f32[2048,8,128]{2,0,1:T(8,128)} fusion(f32[2048,8,128]{2,0,1:T(8,128)} %get-tuple-element.224, s32[4]{0:T(128)S(1)} %fusion.34, f32[4,2048,128]{2,1,0:T(8,128)} %fusion.37), kind=kCustom, calls=%fused_computation.1.clone.1 | custom fusion | flops 1048576 | bytes 12582928 | tf_op jit(solution)/shard_map/while/body/eval_jaxpr/scatter-add | solution.py:57
  361.0 9.0 %scatter_fusion = f32[2048,8,128]{2,0,1:T(8,128)} fusion(f32[2048,8,128]{2,0,1:T(8,128)} %get-tuple-element.224, s32[4]{0:T(128)S(1)} %fusion.34, f32[4,2048,128]{2,1,0:T(8,128)} %fusion.37), kind=kCustom, calls=%fused_computation.1.clone.1 | custom fusion | flops 1048576 | bytes 12582928 | tf_op jit(solution)/shard_map/while/body/eval_jaxpr/scatter-add | solution.py:57
  381.7 9.0 %scatter_fusion = f32[2048,8,128]{2,0,1:T(8,128)} fusion(f32[2048,8,128]{2,0,1:T(8,128)} %get-tuple-element.224, s32[4]{0:T(128)S(1)} %fusion.34, f32[4,2048,128]{2,1,0:T(8,128)} %fusion.37), kind=kCustom, calls=%fused_computation.1.clone.1 | custom fusion | flops 1048576 | bytes 12582928 | tf_op jit(solution)/shard_map/while/body/eval_jaxpr/scatter-add | solution.py:57
  402.4 9.0 %scatter_fusion = f32[2048,8,128]{2,0,1:T(8,128)} fusion(f32[2048,8,128]{2,0,1:T(8,128)} %get-tuple-element.224, s32[4]{0:T(128)S(1)} %fusion.34, f32[4,2048,128]{2,1,0:T(8,128)} %fusion.37), kind=kCustom, calls=%fused_computation.1.clone.1 | custom fusion | flops 1048576 | bytes 12582928 | tf_op jit(solution)/shard_map/while/body/eval_jaxpr/scatter-add | solution.py:57
  423.1 9.0 %scatter_fusion = f32[2048,8,128]{2,0,1:T(8,128)} fusion(f32[2048,8,128]{2,0,1:T(8,128)} %get-tuple-element.224, s32[4]{0:T(128)S(1)} %fusion.34, f32[4,2048,128]{2,1,0:T(8,128)} %fusion.37), kind=kCustom, calls=%fused_computation.1.clone.1 | custom fusion | flops 1048576 | bytes 12582928 | tf_op jit(solution)/shard_map/while/body/eval_jaxpr/scatter-add | solution.py:57
  464.2 8.7 %scatter_fusion = f32[2048,8,128]{2,0,1:T(8,128)} fusion(f32[2048,8,128]{2,0,1:T(8,128)} %get-tuple-element.224, s32[4]{0:T(128)S(1)} %fusion.34, f32[4,2048,128]{2,1,0:T(8,128)} %fusion.37), kind=kCustom, calls=%fused_computation.1.clone.1 | custom fusion | flops 1048576 | bytes 12582928 | tf_op jit(solution)/shard_map/while/body/eval_jaxpr/scatter-add | solution.py:57
  505.0 8.9 %scatter_fusion = f32[2048,8,128]{2,0,1:T(8,128)} fusion(f32[2048,8,128]{2,0,1:T(8,128)} %get-tuple-element.224, s32[4]{0:T(128)S(1)} %fusion.34, f32[4,2048,128]{2,1,0:T(8,128)} %fusion.37), kind=kCustom, calls=%fused_computation.1.clone.1 | custom fusion | flops 1048576 | bytes 12582928 | tf_op jit(solution)/shard_map/while/body/eval_jaxpr/scatter-add | solution.py:57
  546.0 9.1 %scatter_fusion = f32[2048,8,128]{2,0,1:T(8,128)} fusion(f32[2048,8,128]{2,0,1:T(8,128)} %get-tuple-element.224, s32[4]{0:T(128)S(1)} %fusion.34, f32[4,2048,128]{2,1,0:T(8,128)} %fusion.37), kind=kCustom, calls=%fused_computation.1.clone.1 | custom fusion | flops 1048576 | bytes 12582928 | tf_op jit(solution)/shard_map/while/body/eval_jaxpr/scatter-add | solution.py:57
  566.8 8.7 %scatter_fusion = f32[2048,8,128]{2,0,1:T(8,128)} fusion(f32[2048,8,128]{2,0,1:T(8,128)} %get-tuple-element.224, s32[4]{0:T(128)S(1)} %fusion.34, f32[4,2048,128]{2,1,0:T(8,128)} %fusion.37), kind=kCustom, calls=%fused_computation.1.clone.1 | custom fusion | flops 1048576 | bytes 12582928 | tf_op jit(solution)/shard_map/while/body/eval_jaxpr/scatter-add | solution.py:57
  587.2 9.0 %scatter_fusion = f32[2048,8,128]{2,0,1:T(8,128)} fusion(f32[2048,8,128]{2,0,1:T(8,128)} %get-tuple-element.224, s32[4]{0:T(128)S(1)} %fusion.34, f32[4,2048,128]{2,1,0:T(8,128)} %fusion.37), kind=kCustom, calls=%fused_computation.1.clone.1 | custom fusion | flops 1048576 | bytes 12582928 | tf_op jit(solution)/shard_map/while/body/eval_jaxpr/scatter-add | solution.py:57
  608.7 20.7 %collective-permute-done.2 = f32[2048,2,128]{2,0,1:T(8,128)S(1)} collective-permute-done((f32[2048,2,128]{2,0,1:T(8,128)S(1)}, f32[2048,2,128]{2,0,1:T(8,128)S(1)}, u32[]{:S(2)}, u32[]{:S(2)}) %collective-permute-start.2) | collective-permute-done | bytes 2097184 | tf_op jit(solution)/shard_map/ppermute | solution.py:25
  (249 shorter events, 421.6 us)
Async XLA Ops:
  1.1 8.1 %collective-permute-start = (bf16[256,512]{1,0:T(8,128)(2,1)S(1)}, bf16[256,512]{1,0:T(8,128)(2,1)S(1)}, u32[]{:S(2)}, u32[]{:S(2)}) collective-permute-start(bf16[256,512]{1,0:T(8,128)(2,1)S(1)} %get-tuple-element.170), channel_id=1, source_target_pairs={{0,16},{16,32},{32,48},{48,64},{64,80},{80,96},{96,112},{1,17},{17... | collective-permute-start | bytes 786440 | tf_op jit(solution)/shard_map/ppermute | solution.py:14
  4.2 8.8 %collective-permute-start.1 = (bf16[256,512]{1,0:T(8,128)(2,1)S(1)}, bf16[256,512]{1,0:T(8,128)(2,1)S(1)}, u32[]{:S(2)}, u32[]{:S(2)}) collective-permute-start(bf16[256,512]{1,0:T(8,128)(2,1)S(1)} %get-tuple-element.171), channel_id=1, source_target_pairs={{16,0},{32,16},{48,32},{64,48},{80,64},{96,80},{112,96},{17,1},{33... | collective-permute-start | bytes 786440 | tf_op jit(solution)/shard_map/ppermute | solution.py:17
  596.2 12.2 %copy-start = (f32[2048,8,128]{2,0,1:T(8,128)S(1)}, f32[2048,8,128]{2,0,1:T(8,128)}, u32[]{:S(2)}) copy-start(f32[2048,8,128]{2,0,1:T(8,128)} %get-tuple-element.153) | copy-start | bytes 25165828
  598.9 30.5 %collective-permute-start.2 = (f32[2048,2,128]{2,0,1:T(8,128)S(1)}, f32[2048,2,128]{2,0,1:T(8,128)S(1)}, u32[]{:S(2)}, u32[]{:S(2)}) collective-permute-start(f32[2048,2,128]{2,0,1:T(8,128)S(1)} %get-tuple-element.169), channel_id=1, source_target_pairs={{0,1},{1,2},{2,3},{3,4},{4,5},{5,6},{6,7},{7,8},{8,9},{9,10},{10,1... | collective-permute-start | bytes 6291464 | tf_op jit(solution)/shard_map/ppermute | solution.py:25
  606.5 31.0 %collective-permute-start.3 = (f32[2048,2,128]{2,0,1:T(8,128)S(1)}, f32[2048,2,128]{2,0,1:T(8,128)S(1)}, u32[]{:S(2)}, u32[]{:S(2)}) collective-permute-start(f32[2048,2,128]{2,0,1:T(8,128)S(1)} %get-tuple-element.168), channel_id=1, source_target_pairs={{1,0},{2,1},{3,2},{4,3},{5,4},{6,5},{7,6},{8,7},{9,8},{10,9},{11,1... | collective-permute-start | bytes 6291464 | tf_op jit(solution)/shard_map/ppermute | solution.py:25
where the time goes:
time: 647 us; the launch traced here: 639 us
  other arithmetic  256 us (40%)
  matrix products  187 us (29%)
  local copies, waits for them, and re-layouts  147 us (23%)
  waiting for transfers between devices  34.4 us (5%)
  starting transfers between devices  13.9 us (2%)
    scatter-add x28, other arithmetic, apply_term(): return totals.at[:, target_index[term_index]].add(contrib)  248 us
    dot_general x28, matrix products, apply_term(): jnp.einsum('mjc,jce->mje', inner, right_blocks[term_index], preferred_ele...  99.6 us
    dot_general x28, matrix products, apply_term(): jnp.einsum('irc,icm->irm', left_blocks[term_index], picked, preferred_ele...  87.8 us
    reshape x28, local copies, waits for them, and re-layouts, apply_term(): inner.astype(jnp.bfloat16).reshape(local_rows, right_count, block_size)  71.3 us
    gather x28, local copies, waits for them, and re-layouts, apply_term(): picked = jnp.take(source_blocks, source_index[term_index], axis=0)  67.8 us
    ppermute x2, waiting for transfers between devices, from_behind(): return lax.ppermute(array, axis, pairs)  28.5 us
  transfers between devices with their start and end apart: 4, of which 4 were waited for; matrix products, arithmetic and copies ran while one was open for 0% of the time, Pallas kernels for 0%

commit v1 on v0

v1 whole, which is shorter than its diff:
```python
import functools

import jax
import jax.numpy as jnp
from jax import lax
from jax.experimental import pallas as pl
from jax.experimental.pallas import tpu as pltpu
from jax.sharding import PartitionSpec as P

SPAN = 2
B = 128
GROUP = 4
CHUNK = 4
MESH = pl.DeviceIdType.MESH
BF = jnp.bfloat16
F32 = jnp.float32


def max_groups(entries, targets):
    return (entries + (GROUP - 1) * targets) // GROUP


def plan_kernel(terms, right_count, dst_ref, entry_ref, factor_ref, joined_ref, last_ref, count, bucket):
    start = lax.axis_index("rb") * right_count
    targets = right_count + 2 * SPAN
    entries = terms * right_count
    groups = max_groups(entries, targets)
    for d in range(targets):
        count[d] = 0

    def place(w, carry):
        for j in range(right_count):
            d = dst_ref[w, start + j] - start + SPAN
            n = count[d]
            bucket[d * entries + n] = w * right_count + j
            count[d] = n + 1
        return carry

    lax.fori_loop(0, terms, place, 0)

    def blank(g, carry):
        for q in range(GROUP):
            entry_ref[GROUP * g + q] = 0
            factor_ref[GROUP * g + q] = entries
        joined_ref[g] = 0
        return carry

    used = jnp.int32(0)
    for d in range(targets):
        n = count[d]
        parts = (n + GROUP - 1) // GROUP

        def emit(k, g):
            for q in range(GROUP):
                at = GROUP * k + q
                here = at < n
                e = bucket[d * entries + jnp.minimum(at, entries - 1)]
                entry_ref[GROUP * g + q] = jnp.where(here, e, 0)
                factor_ref[GROUP * g + q] = jnp.where(here, e, entries)
            joined_ref[g] = (k > 0).astype(jnp.int32)
            return g + 1

        used = lax.fori_loop(0, parts, emit, used)
        last_ref[d] = jnp.where(n > 0, used - 1, groups)
    lax.fori_loop(used, groups, blank, 0)


def main_kernel(
    sizes, src_ref, entry_ref, factor_ref, joined_ref, last_ref, psi, left, right, out,
    psi_v, low_v, high_v, psi_t, right_v, right_t, left_v, inner, slots,
    send_down, send_up, from_below, from_above, out_v,
    psi_sem, right_sem, left_sem, out_sem, halo_send, halo_recv, edge_send, edge_recv,
):
    lb_size, rb_size, terms, left_count, right_count = sizes
    targets = right_count + 2 * SPAN
    entries = terms * right_count
    groups = max_groups(entries, targets)
    rows, cols = left_count * B, right_count * B
    width = CHUNK * B
    chunks = left_count // CHUNK
    halo = SPAN * B
    a, b = lax.axis_index("lb"), lax.axis_index("rb")
    neighbours = (
        (a > 0, {"lb": a - 1}), (a < lb_size - 1, {"lb": a + 1}),
        (b > 0, {"rb": b - 1}), (b < rb_size - 1, {"rb": b + 1}),
    )

    psi_copy = pltpu.make_async_copy(psi, psi_v, psi_sem)
    right_copy = pltpu.make_async_copy(right, right_v, right_sem)

    def rows_of(c, p):
        return pl.multiple_of(lax.rem(halo + c * width + p * 2 * B, rows), 2 * B)

    def left_copy(c, p):
        return pltpu.make_async_copy(
            left.at[:, pl.ds(rows_of(c, p), 2 * B)],
            left_v.at[lax.rem(c, 2), :, pl.ds(p * 2 * B, 2 * B)],
            left_sem.at[lax.rem(c, 2), p],
        )

    def out_copy(c, p):
        at = pl.ds(rows_of(c, p), 2 * B)
        return pltpu.make_async_copy(out_v.at[at], out.at[at], out_sem.at[c, p])

    def halo_copy(side):
        if side == 0:
            return pltpu.make_async_remote_copy(
                src_ref=psi.at[pl.ds(0, halo)], dst_ref=high_v, send_sem=halo_send.at[0],
                recv_sem=halo_recv.at[0], device_id={"lb": a - 1}, device_id_type=MESH)
        return pltpu.make_async_remote_copy(
            src_ref=psi.at[pl.ds(rows - halo, halo)], dst_ref=low_v, send_sem=halo_send.at[1],
            recv_sem=halo_recv.at[1], device_id={"lb": a + 1}, device_id_type=MESH)

    def edge_copy(c, side):
        if side == 0:
            return pltpu.make_async_remote_copy(
                src_ref=send_down.at[c], dst_ref=from_above.at[c], send_sem=edge_send.at[0, c],
                recv_sem=edge_recv.at[0, c], device_id={"rb": b - 1}, device_id_type=MESH)
        return pltpu.make_async_remote_copy(
            src_ref=send_up.at[c], dst_ref=from_below.at[c], send_sem=edge_send.at[1, c],
            recv_sem=edge_recv.at[1, c], device_id={"rb": b + 1}, device_id_type=MESH)

    psi_copy.start()
    right_copy.start()
    for p in range(2):
        left_copy(0, p).start()

    barrier = pltpu.get_barrier_semaphore()
    for there, device in neighbours:
        @pl.when(there)
        def _():
            pl.semaphore_signal(barrier, inc=1, device_id=device, device_id_type=MESH)
    pl.semaphore_wait(barrier, sum(there.astype(jnp.int32) for there, _ in neighbours))

    @pl.when(a > 0)
    def _():
        halo_copy(0).start()

    @pl.when(a < lb_size - 1)
    def _():
        halo_copy(1).start()

    @pl.when(b == 0)
    def _():
        from_below[...] = jnp.zeros_like(from_below)

    @pl.when(b == rb_size - 1)
    def _():
        from_above[...] = jnp.zeros_like(from_above)

    right_t[entries] = jnp.zeros((B, B), BF)
    slots[groups] = jnp.zeros((B, width), F32)

    psi_copy.wait()

    def turn_psi(s, carry):
        for u in range(4):
            at = pl.multiple_of((4 * s + u) * B, B)
            psi_t[4 * s + u + SPAN] = psi_v[pl.ds(at, B), :].T
        return carry

    lax.fori_loop(0, left_count // 4, turn_psi, 0)
    right_copy.wait()

    def turn_right(w, carry):
        for u in range(4):
            for j in range(right_count):
                right_t[(4 * w + u) * right_count + j] = right_v[4 * w + u, pl.ds(j * B, B), :].T
        return carry

    lax.fori_loop(0, terms // 4, turn_right, 0)

    zero = jnp.zeros((B, B), BF)

    def finish(c):
        @pl.when(b > 0)
        def _():
            edge_copy(c, 1).wait_recv()

        @pl.when(b < rb_size - 1)
        def _():
            edge_copy(c, 0).wait_recv()

        for j in range(right_count):
            mine = slots[last_ref[SPAN + j]]
            if j < SPAN:
                mine = mine + from_below[c, pl.ds(j * B, B), :].astype(F32)
            if j >= right_count - SPAN:
                mine = mine + from_above[c, pl.ds((j - right_count + SPAN) * B, B), :].astype(F32)
            turned = mine.astype(BF).T
            for p in range(2):
                out_v[pl.ds(rows_of(c, p), 2 * B), pl.ds(j * B, B)] = turned[p * 2 * B : (p + 1) * 2 * B]
        for p in range(2):
            out_copy(c, p).start()

    def step(c, carry):
        for p in range(2):
            left_copy(c, p).wait()

        @pl.when(c < chunks - 1)
        def _():
            for p in range(2):
                left_copy(c + 1, p).start()

        @pl.when(c == chunks - 1)
        def _():
            @pl.when(a > 0)
            def _():
                halo_copy(1).wait_recv()
                for k in range(SPAN):
                    psi_t[k] = low_v[pl.ds(k * B, B), :].T

            @pl.when(a < lb_size - 1)
            def _():
                halo_copy(0).wait_recv()
                for k in range(SPAN):
                    psi_t[SPAN + left_count + k] = high_v[pl.ds(k * B, B), :].T

        first = a * left_count
        slot = lax.rem(c, 2)
        for w in range(terms):
            for p in range(2):
                i = first + lax.rem(SPAN + c * CHUNK + 2 * p, left_count)
                shift = SPAN - first
                x = jnp.concatenate(
                    [psi_t[jnp.clip(src_ref[w, i + k] + shift, 0, left_count + 2 * SPAN - 1)] for k in range(2)],
                    axis=1)
                upper = left_v[slot, w, pl.ds(p * 2 * B, B), :].T
                lower = left_v[slot, w, pl.ds(p * 2 * B + B, B), :].T
                both = jnp.concatenate(
                    [jnp.concatenate([upper, zero], axis=1), jnp.concatenate([zero, lower], axis=1)], axis=0)
                y = jnp.dot(x, both, preferred_element_type=F32).astype(BF)
                for j in range(right_count):
                    inner[w * right_count + j, :, pl.ds(p * 2 * B, 2 * B)] = y[j * B : (j + 1) * B]

        @pl.when(c > 0)
        def _():
            finish(c - 1)

        for g in range(groups):
            k = jnp.concatenate([inner[entry_ref[GROUP * g + q]] for q in range(GROUP)], axis=0)
            r = jnp.concatenate([right_t[factor_ref[GROUP * g + q]] for q in range(GROUP)], axis=1)
            y = jnp.dot(r, k, preferred_element_type=F32)
            if g > 0:
                y = y + jnp.where(joined_ref[g] == 1, slots[g - 1], 0.0)
            slots[g] = y
        for k in range(SPAN):
            send_down[c, pl.ds(k * B, B), :] = slots[last_ref[k]].astype(BF)
            send_up[c, pl.ds(k * B, B), :] = slots[last_ref[SPAN + right_count + k]].astype(BF)

        @pl.when(b > 0)
        def _():
            edge_copy(c, 0).start()

        @pl.when(b < rb_size - 1)
        def _():
            edge_copy(c, 1).start()
        return carry

    lax.fori_loop(0, chunks, step, 0)
    finish(chunks - 1)

    def drain(c, carry):
        for p in range(2):
            out_copy(c, p).wait()

        @pl.when(b > 0)
        def _():
            edge_copy(c, 0).wait_send()

        @pl.when(b < rb_size - 1)
        def _():
            edge_copy(c, 1).wait_send()
        return carry

    lax.fori_loop(0, chunks, drain, 0)

    @pl.when(a > 0)
    def _():
        halo_copy(0).wait_send()

    @pl.when(a < lb_size - 1)
    def _():
        halo_copy(1).wait_send()


def on_device(lb_size, rb_size, psi, left_env, right_env, left_src, right_dst):
    rows, cols = psi.shape
    terms = left_env.shape[0]
    left_count, right_count = rows // B, cols // B
    entries, targets = terms * right_count, right_count + 2 * SPAN
    groups = max_groups(entries, targets)
    chunks, width, halo = left_count // CHUNK, CHUNK * B, SPAN * B
    smem = pl.BlockSpec(memory_space=pltpu.SMEM)
    hbm = pl.BlockSpec(memory_space=pl.ANY)
    ints = lambda n: jax.ShapeDtypeStruct((n,), jnp.int32)
    plan = pl.pallas_call(
        functools.partial(plan_kernel, terms, right_count),
        out_shape=(ints(GROUP * groups), ints(GROUP * groups), ints(groups), ints(targets)),
        in_specs=[smem],
        out_specs=(smem,) * 4,
        scratch_shapes=[pltpu.SMEM((targets,), jnp.int32), pltpu.SMEM((targets * entries,), jnp.int32)],
        name="plan",
    )(right_dst)
    dma = pltpu.SemaphoreType.DMA
    return pl.pallas_call(
        functools.partial(main_kernel, (lb_size, rb_size, terms, left_count, right_count)),
        out_shape=jax.ShapeDtypeStruct((rows, cols), BF),
        in_specs=[smem] * 5 + [hbm] * 3,
        out_specs=hbm,
        scratch_shapes=[
            pltpu.VMEM((rows, cols), BF),
            pltpu.VMEM((halo, cols), BF),
            pltpu.VMEM((halo, cols), BF),
            pltpu.VMEM((left_count + 2 * SPAN, cols, B), BF),
            pltpu.VMEM((terms, cols, B), BF),
            pltpu.VMEM((entries + 1, B, B), BF),
            pltpu.VMEM((2, terms, width, B), BF),
            pltpu.VMEM((entries, B, width), BF),
            pltpu.VMEM((groups + 1, B, width), F32),
            pltpu.VMEM((chunks, halo, width), BF),
            pltpu.VMEM((chunks, halo, width), BF),
            pltpu.VMEM((chunks, halo, width), BF),
            pltpu.VMEM((chunks, halo, width), BF),
            pltpu.VMEM((rows, cols), BF),
            dma(()), dma(()), dma((2, 2)), dma((chunks, 2)), dma((2,)), dma((2,)), dma((2, chunks)), dma((2, chunks)),
        ],
        compiler_params=pltpu.CompilerParams(
            collective_id=0, has_side_effects=True, vmem_limit_bytes=60 * 2**20),
        name="apply",
    )(left_src, *plan, psi, left_env, right_env)


def solution(mesh):
    return jax.shard_map(
        functools.partial(on_device, mesh.shape["lb"], mesh.shape["rb"]),
        mesh=mesh,
        in_specs=(P("lb", "rb"), P(None, "lb", None), P(None, "rb", None), P(), P()),
        out_specs=P("lb", "rb"),
        check_vma=False,
    )
```

time: 647 us -> 56.4 us (0.09); the launches traced: 639 us -> 56.1 us
  other arithmetic: 256 us -> 0 us
  matrix products: 187 us -> 0 us
  local copies, waits for them, and re-layouts: 147 us -> 3.05 us
  Pallas kernels: 0 us -> 53.1 us
  waiting for transfers between devices: 34.4 us -> 0 us
  starting transfers between devices: 13.9 us -> 0 us
    scatter-add x30 -> x0, other arithmetic: 248 us -> none  [the longest x28 248 us: apply_term(): return totals.at[:, target_index[term_index]].add(contrib)]
    dot_general x56 -> x0, matrix products: 187 us -> none  [the longest x28 99.6 us: apply_term(): jnp.einsum('mjc,jce->mje', inner, right_blocks[term_index], preferred_ele...]
    reshape x28 -> x0, local copies, waits for them, and re-layouts: 71.3 us -> none  [apply_term(): inner.astype(jnp.bfloat16).reshape(local_rows, right_count, block_size)]
    gather x28 -> x0, local copies, waits for them, and re-layouts: 67.8 us -> none  [apply_term(): picked = jnp.take(source_blocks, source_index[term_index], axis=0)]
    pallas_call x0 -> x2, Pallas kernels: none -> 53.1 us  [the longest x1 50.1 us: on_device(): pl.pallas_call(functools.partial(main_kernel, (lb_size, rb_size, terms, l...]
    ppermute x4 -> x0, waiting for transfers between devices: 34.4 us -> none  [the longest x2 28.5 us: from_behind(): return lax.ppermute(array, axis, pairs)]
    ppermute x4 -> x0, starting transfers between devices: 13.9 us -> none  [the longest x2 9.47 us: from_behind(): return lax.ppermute(array, axis, pairs)]
  transfers between devices with their start and end apart: 4 -> 0, of which waited for: 4 -> 0; matrix products, arithmetic and copies ran while one was open for 0% -> 0% of each run, Pallas kernels for 0% -> 0%
where the time goes in v1:
time: 56.4 us; the launch traced here: 56.1 us
  Pallas kernels  53.1 us (94%)
  local copies, waits for them, and re-layouts  3.05 us (5%)
    pallas_call x1, Pallas kernels, on_device(): pl.pallas_call(functools.partial(main_kernel, (lb_size, rb_size, terms, l...  50.1 us
    unnamed x1, local copies, waits for them, and re-layouts  3.05 us
    pallas_call x1, Pallas kernels, on_device(): pl.pallas_call(functools.partial(plan_kernel, terms, right_count), out_sh...  2.93 us

profile of v1, /device:TPU:25, one launch (start us, length us, event | category | flops | bytes accessed | tf_op | source)
XLA Modules:
  0.0 56.1 jit_solution(17877594473754549811)
XLA Ops:
  0.0 2.9 %plan.1 = (s32[136]{0:T(256)}, s32[136]{0:T(256)}, s32[34]{0:T(128)}, s32[8]{0:T(128)}) custom-call(s32[28,64]{1,0:T(8,128)} %dst_ref.1), custom_call_target="tpu_custom_call" | custom-call | tf_op jit(solution)/shard_map/plan/pallas_call | solution.py:297
  2.9 50.1 %apply.1 = bf16[2048,512]{1,0:T(8,128)(2,1)} custom-call(s32[28,128]{1,0:T(8,128)} %src_ref.1, s32[136]{0:T(256)} %get-tuple-element.9.entry_ref, s32[136]{0:T(256)} %get-tuple-element.10.factor_ref, s32[34]{0:T(128)} %get-tuple-element.11.joined_ref, s32[8]{0:T(128)} %get-tuple-element.12.last_ref, bf16[2048,512]{1,0:T(8,128)(2,1)} %psi.1, ...), custom_call_target="tpu_custom_call" | custom-call | tf_op jit(solution)/shard_map/apply/pallas_call | solution.py:306
  53.1 3.0 %copy.7 = bf16[2048,512]{1,0:T(8,128)(2,1)} copy(bf16[2048,512]{1,0:T(8,128)(2,1)} %apply.1) | data formatting | bytes 4194304

commit v2 on v1

v2 whole, which is shorter than its diff:
```python
import functools

import jax
import jax.numpy as jnp
from jax import lax
from jax.experimental import pallas as pl
from jax.experimental.pallas import tpu as pltpu
from jax.sharding import PartitionSpec as P

SPAN = 2
B = 128
GROUP = 4
CHUNK = 4
LISTED = 256
MESH = pl.DeviceIdType.MESH
BF = jnp.bfloat16
F32 = jnp.float32


def max_groups(entries, targets):
    return (entries + (GROUP - 1) * targets) // GROUP


def plan(terms, right_count, start, dst_ref, list_v, last_ref):
    targets = right_count + 2 * SPAN
    entries = terms * right_count
    groups = max_groups(entries, targets)

    def target(w, j):
        return dst_ref[w, start + j] - start + SPAN

    def tally(w, counts):
        for j in range(right_count):
            d = target(w, j)
            counts = tuple(n + (d == k).astype(jnp.int32) for k, n in enumerate(counts))
        return counts

    zeros = (jnp.int32(0),) * targets
    counts = lax.fori_loop(0, terms, tally, zeros)
    place = lax.broadcasted_iota(jnp.int32, (8, B), 0) * B + lax.broadcasted_iota(jnp.int32, (8, B), 1)
    listed = jnp.where(place < LISTED, entries, 1)
    begin = jnp.int32(0)
    begins = []
    for k, n in enumerate(counts):
        begins.append(begin * GROUP)
        listed = jnp.where(place == LISTED + begin, 0, listed)
        begin = begin + (n + GROUP - 1) // GROUP
        last_ref[k] = jnp.where(n > 0, begin - 1, groups)

    def put(w, carry):
        nexts, listed = carry
        for j in range(right_count):
            d = target(w, j)
            at = sum(jnp.where(d == k, n, 0) for k, n in enumerate(nexts))
            nexts = tuple(n + (d == k).astype(jnp.int32) for k, n in enumerate(nexts))
            listed = jnp.where(place == at, w * right_count + j, listed)
        return nexts, listed

    _, listed = lax.fori_loop(0, terms, put, (tuple(begins), listed))
    list_v[...] = listed


def main_kernel(
    sizes, src_ref, dst_ref, psi, left, right, out,
    list_v, list_s, last_ref, psi_v, low_v, high_v, psi_t, right_v, right_t, left_v, inner, slots, held,
    send_down, send_up, from_below, from_above,
    list_sem, psi_sem, right_sem, left_sem, halo_send, halo_recv, edge_send, edge_recv,
):
    lb_size, rb_size, terms, left_count, right_count = sizes
    targets = right_count + 2 * SPAN
    entries = terms * right_count
    groups = max_groups(entries, targets)
    rows, cols = left_count * B, right_count * B
    width = CHUNK * B
    chunks = left_count // CHUNK
    halo = SPAN * B
    a, b = lax.axis_index("lb"), lax.axis_index("rb")
    neighbours = (
        (a > 0, {"lb": a - 1}), (a < lb_size - 1, {"lb": a + 1}),
        (b > 0, {"rb": b - 1}), (b < rb_size - 1, {"rb": b + 1}),
    )

    psi_copy = pltpu.make_async_copy(psi, psi_v, psi_sem)
    right_copy = pltpu.make_async_copy(right, right_v, right_sem)
    list_copy = pltpu.make_async_copy(list_v, list_s, list_sem)

    def rows_of(c, p):
        return pl.multiple_of(lax.rem(halo + c * width + p * 2 * B, rows), 2 * B)

    def left_copy(c, p):
        return pltpu.make_async_copy(
            left.at[:, pl.ds(rows_of(c, p), 2 * B)],
            left_v.at[lax.rem(c, 2), :, pl.ds(p * 2 * B, 2 * B)],
            left_sem.at[lax.rem(c, 2), p],
        )

    def halo_copy(side):
        if side == 0:
            return pltpu.make_async_remote_copy(
                src_ref=psi.at[pl.ds(0, halo)], dst_ref=high_v, send_sem=halo_send.at[0],
                recv_sem=halo_recv.at[0], device_id={"lb": a - 1}, device_id_type=MESH)
        return pltpu.make_async_remote_copy(
            src_ref=psi.at[pl.ds(rows - halo, halo)], dst_ref=low_v, send_sem=halo_send.at[1],
            recv_sem=halo_recv.at[1], device_id={"lb": a + 1}, device_id_type=MESH)

    def edge_copy(c, p, side):
        if side == 0:
            return pltpu.make_async_remote_copy(
                src_ref=send_down.at[c, p], dst_ref=from_above.at[c, p], send_sem=edge_send.at[0, c, p],
                recv_sem=edge_recv.at[0, c, p], device_id={"rb": b - 1}, device_id_type=MESH)
        return pltpu.make_async_remote_copy(
            src_ref=send_up.at[c, p], dst_ref=from_below.at[c, p], send_sem=edge_send.at[1, c, p],
            recv_sem=edge_recv.at[1, c, p], device_id={"rb": b + 1}, device_id_type=MESH)

    psi_copy.start()
    right_copy.start()
    for p in range(2):
        left_copy(0, p).start()

    barrier = pltpu.get_barrier_semaphore()
    for there, device in neighbours:
        @pl.when(there)
        def _():
            pl.semaphore_signal(barrier, inc=1, device_id=device, device_id_type=MESH)
    plan(terms, right_count, b * right_count, dst_ref, list_v, last_ref)
    list_copy.start()
    pl.semaphore_wait(barrier, sum(there.astype(jnp.int32) for there, _ in neighbours))

    @pl.when(a > 0)
    def _():
        halo_copy(0).start()

    @pl.when(a < lb_size - 1)
    def _():
        halo_copy(1).start()

    @pl.when(b == 0)
    def _():
        from_below[...] = jnp.zeros_like(from_below)

    @pl.when(b == rb_size - 1)
    def _():
        from_above[...] = jnp.zeros_like(from_above)

    right_t[entries] = jnp.zeros((B, B), BF)
    slots[groups] = jnp.zeros((B, 2 * B), F32)

    psi_copy.wait()

    def turn_psi(s, carry):
        for u in range(4):
            at = pl.multiple_of((4 * s + u) * B, B)
            psi_t[4 * s + u + SPAN] = psi_v[pl.ds(at, B), :].T
        return carry

    lax.fori_loop(0, left_count // 4, turn_psi, 0)
    right_copy.wait()

    def turn_right(w, carry):
        for u in range(4):
            for j in range(right_count):
                right_t[(4 * w + u) * right_count + j] = right_v[4 * w + u, pl.ds(j * B, B), :].T
        return carry

    lax.fori_loop(0, terms // 4, turn_right, 0)

    zero = jnp.zeros((B, B), BF)

    def finish(c, p):
        @pl.when(b > 0)
        def _():
            edge_copy(c, p, 1).wait_recv()

        @pl.when(b < rb_size - 1)
        def _():
            edge_copy(c, p, 0).wait_recv()

        for j in range(right_count):
            mine = held[p, lax.rem(c, 2), j]
            if j < SPAN:
                mine = mine + from_below[c, p, pl.ds(j * B, B), :].astype(F32)
            if j >= right_count - SPAN:
                mine = mine + from_above[c, p, pl.ds((j - right_count + SPAN) * B, B), :].astype(F32)
            out[pl.ds(rows_of(c, p), 2 * B), pl.ds(j * B, B)] = mine.astype(BF).T

    def step(c, carry):
        for p in range(2):
            left_copy(c, p).wait()

        @pl.when(c < chunks - 1)
        def _():
            for p in range(2):
                left_copy(c + 1, p).start()

        @pl.when(c == chunks - 1)
        def _():
            @pl.when(a > 0)
            def _():
                halo_copy(1).wait_recv()
                for k in range(SPAN):
                    psi_t[k] = low_v[pl.ds(k * B, B), :].T

            @pl.when(a < lb_size - 1)
            def _():
                halo_copy(0).wait_recv()
                for k in range(SPAN):
                    psi_t[SPAN + left_count + k] = high_v[pl.ds(k * B, B), :].T

        first = a * left_count
        slot = lax.rem(c, 2)
        for w in range(terms):
            for p in range(2):
                i = first + lax.rem(SPAN + c * CHUNK + 2 * p, left_count)
                shift = SPAN - first
                x = jnp.concatenate(
                    [psi_t[jnp.clip(src_ref[w, i + k] + shift, 0, left_count + 2 * SPAN - 1)] for k in range(2)],
                    axis=1)
                upper = left_v[slot, w, pl.ds(p * 2 * B, B), :].T
                lower = left_v[slot, w, pl.ds(p * 2 * B + B, B), :].T
                both = jnp.concatenate(
                    [jnp.concatenate([upper, zero], axis=1), jnp.concatenate([zero, lower], axis=1)], axis=0)
                y = jnp.dot(x, both, preferred_element_type=F32).astype(BF)
                for j in range(right_count):
                    inner[w * right_count + j, :, pl.ds(p * 2 * B, 2 * B)] = y[j * B : (j + 1) * B]

        @pl.when(c == 0)
        def _():
            list_copy.wait()

        def pair(n):
            return list_s[n // B, n % B]

        for p in range(2):
            for g in range(groups):
                at = [pair(GROUP * g + q) for q in range(GROUP)]
                k = jnp.concatenate(
                    [inner[jnp.clip(e, 0, entries - 1), :, pl.ds(p * 2 * B, 2 * B)] for e in at], axis=0)
                r = jnp.concatenate([right_t[e] for e in at], axis=1)
                y = jnp.dot(r, k, preferred_element_type=F32)
                if g > 0:
                    y = y + jnp.where(pair(LISTED + g) == 1, slots[g - 1], 0.0)
                slots[g] = y
            for k in range(SPAN):
                send_down[c, p, pl.ds(k * B, B), :] = slots[last_ref[k]].astype(BF)
                send_up[c, p, pl.ds(k * B, B), :] = slots[last_ref[SPAN + right_count + k]].astype(BF)

            @pl.when(b > 0)
            def _():
                edge_copy(c, p, 0).start()

            @pl.when(b < rb_size - 1)
            def _():
                edge_copy(c, p, 1).start()

            for j in range(right_count):
                held[p, slot, j] = slots[last_ref[SPAN + j]]

            @pl.when(c > 0)
            def _():
                finish(c - 1, p)
        return carry

    lax.fori_loop(0, chunks, step, 0)
    for p in range(2):
        finish(chunks - 1, p)

    def drain(c, carry):
        for p in range(2):
            @pl.when(b > 0)
            def _():
                edge_copy(c, p, 0).wait_send()

            @pl.when(b < rb_size - 1)
            def _():
                edge_copy(c, p, 1).wait_send()
        return carry

    lax.fori_loop(0, chunks, drain, 0)

    @pl.when(a > 0)
    def _():
        halo_copy(0).wait_send()

    @pl.when(a < lb_size - 1)
    def _():
        halo_copy(1).wait_send()


def on_device(lb_size, rb_size, psi, left_env, right_env, left_src, right_dst):
    rows, cols = psi.shape
    terms = left_env.shape[0]
    left_count, right_count = rows // B, cols // B
    entries, targets = terms * right_count, right_count + 2 * SPAN
    groups = max_groups(entries, targets)
    chunks, width, halo = left_count // CHUNK, CHUNK * B, SPAN * B
    smem = pl.BlockSpec(memory_space=pltpu.SMEM)
    hbm = pl.BlockSpec(memory_space=pl.ANY)
    dma = pltpu.SemaphoreType.DMA
    edge = pltpu.VMEM((chunks, 2, halo, 2 * B), BF)
    return pl.pallas_call(
        functools.partial(main_kernel, (lb_size, rb_size, terms, left_count, right_count)),
        out_shape=pltpu.VMEM((rows, cols), BF),
        in_specs=[smem] * 2 + [hbm] * 3,
        out_specs=pl.BlockSpec(memory_space=pltpu.VMEM),
        scratch_shapes=[
            pltpu.VMEM((8, B), jnp.int32),
            pltpu.SMEM((8, B), jnp.int32),
            pltpu.SMEM((targets,), jnp.int32),
            pltpu.VMEM((rows, cols), BF),
            pltpu.VMEM((halo, cols), BF),
            pltpu.VMEM((halo, cols), BF),
            pltpu.VMEM((left_count + 2 * SPAN, cols, B), BF),
            pltpu.VMEM((terms, cols, B), BF),
            pltpu.VMEM((entries + 1, B, B), BF),
            pltpu.VMEM((2, terms, width, B), BF),
            pltpu.VMEM((entries, B, width), BF),
            pltpu.VMEM((groups + 1, B, 2 * B), F32),
            pltpu.VMEM((2, 2, right_count, B, 2 * B), F32),
            edge, edge, edge, edge,
            dma(()), dma(()), dma(()), dma((2, 2)), dma((2,)), dma((2,)), dma((2, chunks, 2)), dma((2, chunks, 2)),
        ],
        compiler_params=pltpu.CompilerParams(
            collective_id=0, has_side_effects=True, vmem_limit_bytes=54 * 2**20),
        name="apply",
    )(left_src, right_dst, psi, left_env, right_env)


def solution(mesh):
    return jax.shard_map(
        functools.partial(on_device, mesh.shape["lb"], mesh.shape["rb"]),
        mesh=mesh,
        in_specs=(P("lb", "rb"), P(None, "lb", None), P(None, "rb", None), P(), P()),
        out_specs=P("lb", "rb"),
        check_vma=False,
    )
```

time: 56.4 us -> 44.9 us (0.80)
  Pallas kernels: 53.1 us -> 43.2 us
  local copies, waits for them, and re-layouts: 3.05 us -> 1.32 us
    pallas_call x1, Pallas kernels: 50.1 us -> 43.2 us  [on_device(): pl.pallas_call(functools.partial(main_kernel, (lb_size, rb_size, terms, l...]
    pallas_call x1 -> x0, Pallas kernels: 2.93 us -> none  [on_device(): pl.pallas_call(functools.partial(plan_kernel, terms, right_count), out_sh...]
    unnamed x1, local copies, waits for them, and re-layouts: 3.05 us -> 1.32 us
where the time goes in v2:
time: 44.9 us; the launch traced here: 44.5 us
  Pallas kernels  43.2 us (96%)
  local copies, waits for them, and re-layouts  1.32 us (3%)
    pallas_call x1, Pallas kernels, on_device(): pl.pallas_call(functools.partial(main_kernel, (lb_size, rb_size, terms, l...  43.2 us
    unnamed x1, local copies, waits for them, and re-layouts  1.32 us

profile of v2, /device:TPU:25, one launch (start us, length us, event | category | flops | bytes accessed | tf_op | source)
XLA Modules:
  0.0 44.5 jit_solution(14736855621238527902)
XLA Ops:
  0.0 43.2 %apply.1 = bf16[2048,512]{1,0:T(8,128)(2,1)S(1)} custom-call(s32[28,128]{1,0:T(8,128)} %src_ref.1, s32[28,64]{1,0:T(8,128)} %dst_ref.1, bf16[2048,512]{1,0:T(8,128)(2,1)} %psi.1, bf16[28,2048,128]{2,1,0:T(8,128)(2,1)} %left.1, bf16[28,512,128]{2,1,0:T(8,128)(2,1)} %right.1), custom_call_target="tpu_custom_call" | custom-call | tf_op jit(solution)/shard_map/apply/pallas_call | solution.py:300
  43.2 1.3 %copy.7 = bf16[2048,512]{1,0:T(8,128)(2,1)} copy(bf16[2048,512]{1,0:T(8,128)(2,1)S(1)} %apply.1) | data formatting | bytes 4194304

commit v3 on v2

--- a/solution.py
+++ b/solution.py
@@ -9,7 +9,7 @@
 
 SPAN = 2
 B = 128
-GROUP = 4
+GROUP = 2
 CHUNK = 4
 LISTED = 256
 MESH = pl.DeviceIdType.MESH
@@ -32,7 +32,8 @@
     def tally(w, counts):
         for j in range(right_count):
             d = target(w, j)
-            counts = tuple(n + (d == k).astype(jnp.int32) for k, n in enumerate(counts))
+            counts = tuple(
+                jnp.where(d == k, n + 1, n) if j <= k <= j + 2 * SPAN else n for k, n in enumerate(counts))
         return counts
 
     zeros = (jnp.int32(0),) * targets
@@ -51,8 +52,11 @@
         nexts, listed = carry
         for j in range(right_count):
             d = target(w, j)
-            at = sum(jnp.where(d == k, n, 0) for k, n in enumerate(nexts))
-            nexts = tuple(n + (d == k).astype(jnp.int32) for k, n in enumerate(nexts))
+            at = nexts[j]
+            for k in range(j + 1, j + 2 * SPAN + 1):
+                at = jnp.where(d == k, nexts[k], at)
+            nexts = tuple(
+                jnp.where(d == k, n + 1, n) if j <= k <= j + 2 * SPAN else n for k, n in enumerate(nexts))
             listed = jnp.where(place == at, w * right_count + j, listed)
         return nexts, listed
 
@@ -61,10 +65,10 @@
 
 
 def main_kernel(
-    sizes, src_ref, dst_ref, psi, left, right, out,
-    list_v, list_s, last_ref, psi_v, low_v, high_v, psi_t, right_v, right_t, left_v, inner, slots, held,
+    sizes, src, dst, psi, left, right, out,
+    src_ref, dst_ref, list_v, list_s, last_ref, low_v, high_v, psi_t, right_t, left_v, inner, slots,
     send_down, send_up, from_below, from_above,
-    list_sem, psi_sem, right_sem, left_sem, halo_send, halo_recv, edge_send, edge_recv,
+    index_sem, list_sem, psi_sem, right_sem, left_sem, halo_send, halo_recv, edge_send, edge_recv,
 ):
     lb_size, rb_size, terms, left_count, right_count = sizes
     targets = right_count + 2 * SPAN
@@ -80,8 +84,10 @@
         (b > 0, {"rb": b - 1}), (b < rb_size - 1, {"rb": b + 1}),
     )
 
-    psi_copy = pltpu.make_async_copy(psi, psi_v, psi_sem)
-    right_copy = pltpu.make_async_copy(right, right_v, right_sem)
+    psi_copy = pltpu.make_async_copy(psi, out, psi_sem)
+    src_copy = pltpu.make_async_copy(src, src_ref, index_sem.at[0])
+    dst_copy = pltpu.make_async_copy(dst, dst_ref, index_sem.at[1])
+    right_copy = pltpu.make_async_copy(right, left_v.at[1], right_sem)
     list_copy = pltpu.make_async_copy(list_v, list_s, list_sem)
 
     def rows_of(c, p):
@@ -112,7 +118,9 @@
             src_ref=send_up.at[c, p], dst_ref=from_below.at[c, p], send_sem=edge_send.at[1, c, p],
             recv_sem=edge_recv.at[1, c, p], device_id={"rb": b + 1}, device_id_type=MESH)
 
+    dst_copy.start()
     psi_copy.start()
+    src_copy.start()
     right_copy.start()
     for p in range(2):
         left_copy(0, p).start()
@@ -122,35 +130,27 @@
         @pl.when(there)
         def _():
             pl.semaphore_signal(barrier, inc=1, device_id=device, device_id_type=MESH)
+    @pl.when(b == 0)
+    def _():
+        from_below[...] = jnp.zeros_like(from_below)
+
+    @pl.when(b == rb_size - 1)
+    def _():
+        from_above[...] = jnp.zeros_like(from_above)
+
+    right_t[entries] = jnp.zeros((B, B), BF)
+    for p in range(2):
+        slots[p, groups] = jnp.zeros((B, 2 * B), F32)
+
+    dst_copy.wait()
     plan(terms, right_count, b * right_count, dst_ref, list_v, last_ref)
     list_copy.start()
-    pl.semaphore_wait(barrier, sum(there.astype(jnp.int32) for there, _ in neighbours))
-
-    @pl.when(a > 0)
-    def _():
-        halo_copy(0).start()
-
-    @pl.when(a < lb_size - 1)
-    def _():
-        halo_copy(1).start()
-
-    @pl.when(b == 0)
-    def _():
-        from_below[...] = jnp.zeros_like(from_below)
-
-    @pl.when(b == rb_size - 1)
-    def _():
-        from_above[...] = jnp.zeros_like(from_above)
-
-    right_t[entries] = jnp.zeros((B, B), BF)
-    slots[groups] = jnp.zeros((B, 2 * B), F32)
-
     psi_copy.wait()
 
     def turn_psi(s, carry):
         for u in range(4):
             at = pl.multiple_of((4 * s + u) * B, B)
-            psi_t[4 * s + u + SPAN] = psi_v[pl.ds(at, B), :].T
+            psi_t[4 * s + u + SPAN] = out[pl.ds(at, B), :].T
         return carry
 
     lax.fori_loop(0, left_count // 4, turn_psi, 0)
@@ -159,10 +159,21 @@
     def turn_right(w, carry):
         for u in range(4):
             for j in range(right_count):
-                right_t[(4 * w + u) * right_count + j] = right_v[4 * w + u, pl.ds(j * B, B), :].T
+                right_t[(4 * w + u) * right_count + j] = left_v[1, 4 * w + u, pl.ds(j * B, B), :].T
         return carry
 
     lax.fori_loop(0, terms // 4, turn_right, 0)
+
+    src_copy.wait()
+    pl.semaphore_wait(barrier, sum(there.astype(jnp.int32) for there, _ in neighbours))
+
+    @pl.when(a > 0)
+    def _():
+        halo_copy(0).start()
+
+    @pl.when(a < lb_size - 1)
+    def _():
+        halo_copy(1).start()
 
     zero = jnp.zeros((B, B), BF)
 
@@ -176,7 +187,7 @@
             edge_copy(c, p, 0).wait_recv()
 
         for j in range(right_count):
-            mine = held[p, lax.rem(c, 2), j]
+            mine = slots[p, last_ref[SPAN + j]]
             if j < SPAN:
                 mine = mine + from_below[c, p, pl.ds(j * B, B), :].astype(F32)
             if j >= right_count - SPAN:
@@ -231,6 +242,10 @@
             return list_s[n // B, n % B]
 
         for p in range(2):
+            @pl.when(c > 0)
+            def _():
+                finish(c - 1, p)
+
             for g in range(groups):
                 at = [pair(GROUP * g + q) for q in range(GROUP)]
                 k = jnp.concatenate(
@@ -238,11 +253,11 @@
                 r = jnp.concatenate([right_t[e] for e in at], axis=1)
                 y = jnp.dot(r, k, preferred_element_type=F32)
                 if g > 0:
-                    y = y + jnp.where(pair(LISTED + g) == 1, slots[g - 1], 0.0)
-                slots[g] = y
+                    y = y + jnp.where(pair(LISTED + g) == 1, slots[p, g - 1], 0.0)
+                slots[p, g] = y
             for k in range(SPAN):
-                send_down[c, p, pl.ds(k * B, B), :] = slots[last_ref[k]].astype(BF)
-                send_up[c, p, pl.ds(k * B, B), :] = slots[last_ref[SPAN + right_count + k]].astype(BF)
+                send_down[c, p, pl.ds(k * B, B), :] = slots[p, last_ref[k]].astype(BF)
+                send_up[c, p, pl.ds(k * B, B), :] = slots[p, last_ref[SPAN + right_count + k]].astype(BF)
 
             @pl.when(b > 0)
             def _():
@@ -252,12 +267,6 @@
             def _():
                 edge_copy(c, p, 1).start()
 
-            for j in range(right_count):
-                held[p, slot, j] = slots[last_ref[SPAN + j]]
-
-            @pl.when(c > 0)
-            def _():
-                finish(c - 1, p)
         return carry
 
     lax.fori_loop(0, chunks, step, 0)
@@ -293,31 +302,29 @@
     entries, targets = terms * right_count, right_count + 2 * SPAN
     groups = max_groups(entries, targets)
     chunks, width, halo = left_count // CHUNK, CHUNK * B, SPAN * B
-    smem = pl.BlockSpec(memory_space=pltpu.SMEM)
     hbm = pl.BlockSpec(memory_space=pl.ANY)
     dma = pltpu.SemaphoreType.DMA
     edge = pltpu.VMEM((chunks, 2, halo, 2 * B), BF)
     return pl.pallas_call(
         functools.partial(main_kernel, (lb_size, rb_size, terms, left_count, right_count)),
         out_shape=pltpu.VMEM((rows, cols), BF),
-        in_specs=[smem] * 2 + [hbm] * 3,
+        in_specs=[hbm] * 5,
         out_specs=pl.BlockSpec(memory_space=pltpu.VMEM),
         scratch_shapes=[
+            pltpu.SMEM(left_src.shape, jnp.int32),
+            pltpu.SMEM(right_dst.shape, jnp.int32),
             pltpu.VMEM((8, B), jnp.int32),
             pltpu.SMEM((8, B), jnp.int32),
             pltpu.SMEM((targets,), jnp.int32),
-            pltpu.VMEM((rows, cols), BF),
             pltpu.VMEM((halo, cols), BF),
             pltpu.VMEM((halo, cols), BF),
             pltpu.VMEM((left_count + 2 * SPAN, cols, B), BF),
-            pltpu.VMEM((terms, cols, B), BF),
             pltpu.VMEM((entries + 1, B, B), BF),
             pltpu.VMEM((2, terms, width, B), BF),
             pltpu.VMEM((entries, B, width), BF),
-            pltpu.VMEM((groups + 1, B, 2 * B), F32),
-            pltpu.VMEM((2, 2, right_count, B, 2 * B), F32),
+            pltpu.VMEM((2, groups + 1, B, 2 * B), F32),
             edge, edge, edge, edge,
-            dma(()), dma(()), dma(()), dma((2, 2)), dma((2,)), dma((2,)), dma((2, chunks, 2)), dma((2, chunks, 2)),
+            dma((2,)), dma(()), dma(()), dma(()), dma((2, 2)), dma((2,)), dma((2,)), dma((2, chunks, 2)), dma((2, chunks, 2)),
         ],
         compiler_params=pltpu.CompilerParams(
             collective_id=0, has_side_effects=True, vmem_limit_bytes=54 * 2**20),

time: 44.9 us -> 43.8 us (0.976)
  Pallas kernels: 43.2 us -> 42.3 us
    pallas_call x1, Pallas kernels: 43.2 us -> 42.3 us  [on_device(): pl.pallas_call(functools.partial(main_kernel, (lb_size, rb_size, terms, l...]
where the time goes in v3:
time: 43.8 us; the launch traced here: 43.7 us
  Pallas kernels  42.3 us (97%)
  local copies, waits for them, and re-layouts  1.32 us (3%)
    pallas_call x1, Pallas kernels, on_device(): pl.pallas_call(functools.partial(main_kernel, (lb_size, rb_size, terms, l...  42.3 us
    unnamed x1, local copies, waits for them, and re-layouts  1.32 us

profile of v3, /device:TPU:25, one launch (start us, length us, event | category | flops | bytes accessed | tf_op | source)
XLA Modules:
  0.0 43.7 jit_solution(11465711107973461756)
XLA Ops:
  0.0 42.3 %apply.1 = bf16[2048,512]{1,0:T(8,128)(2,1)S(1)} custom-call(s32[28,128]{1,0:T(8,128)} %src.1, s32[28,64]{1,0:T(8,128)} %dst.1, bf16[2048,512]{1,0:T(8,128)(2,1)} %psi.1, bf16[28,2048,128]{2,1,0:T(8,128)(2,1)} %left.1, bf16[28,512,128]{2,1,0:T(8,128)(2,1)} %right.1), custom_call_target="tpu_custom_call" | custom-call | tf_op jit(solution)/shard_map/apply/pallas_call | solution.py:308
  42.3 1.3 %copy.7 = bf16[2048,512]{1,0:T(8,128)(2,1)} copy(bf16[2048,512]{1,0:T(8,128)(2,1)S(1)} %apply.1) | data formatting | bytes 4194304

commit v4 on v3

--- a/solution.py
+++ b/solution.py
@@ -21,13 +21,16 @@
     return (entries + (GROUP - 1) * targets) // GROUP
 
 
-def plan(terms, right_count, start, dst_ref, list_v, last_ref):
+def plan(terms, right_count, start, odd, dst_ref, list_v, last_ref):
     targets = right_count + 2 * SPAN
     entries = terms * right_count
     groups = max_groups(entries, targets)
 
+    blocks = [jnp.where(odd, right_count - 1 - j, j) for j in range(right_count)]
+    sign, base = jnp.where(odd, -1, 1), jnp.where(odd, targets - 1 - SPAN + start, SPAN - start)
+
     def target(w, j):
-        return dst_ref[w, start + j] - start + SPAN
+        return base + sign * dst_ref[w, start + blocks[j]]
 
     def tally(w, counts):
         for j in range(right_count):
@@ -57,7 +60,7 @@
                 at = jnp.where(d == k, nexts[k], at)
             nexts = tuple(
                 jnp.where(d == k, n + 1, n) if j <= k <= j + 2 * SPAN else n for k, n in enumerate(nexts))
-            listed = jnp.where(place == at, w * right_count + j, listed)
+            listed = jnp.where(place == at, w * right_count + blocks[j], listed)
         return nexts, listed
 
     _, listed = lax.fori_loop(0, terms, put, (tuple(begins), listed))
@@ -67,7 +70,7 @@
 def main_kernel(
     sizes, src, dst, psi, left, right, out,
     src_ref, dst_ref, list_v, list_s, last_ref, low_v, high_v, psi_t, right_t, left_v, inner, slots,
-    send_down, send_up, from_below, from_above,
+    send_outer, send_inner, arrived,
     index_sem, list_sem, psi_sem, right_sem, left_sem, halo_send, halo_recv, edge_send, edge_recv,
 ):
     lb_size, rb_size, terms, left_count, right_count = sizes
@@ -79,9 +82,13 @@
     chunks = left_count // CHUNK
     halo = SPAN * B
     a, b = lax.axis_index("lb"), lax.axis_index("rb")
+    early = max_groups(SPAN * terms, SPAN)
+    odd = lax.rem(b, 2) == 1
+    outer, inner_b = jnp.where(odd, b + 1, b - 1), jnp.where(odd, b - 1, b + 1)
+    has_outer = (b > 0) & (b < rb_size - 1)
     neighbours = (
         (a > 0, {"lb": a - 1}), (a < lb_size - 1, {"lb": a + 1}),
-        (b > 0, {"rb": b - 1}), (b < rb_size - 1, {"rb": b + 1}),
+        (has_outer, {"rb": outer}), (b >= 0, {"rb": inner_b}),
     )
 
     psi_copy = pltpu.make_async_copy(psi, out, psi_sem)
@@ -109,21 +116,22 @@
             src_ref=psi.at[pl.ds(rows - halo, halo)], dst_ref=low_v, send_sem=halo_send.at[1],
             recv_sem=halo_recv.at[1], device_id={"lb": a + 1}, device_id_type=MESH)
 
-    def edge_copy(c, p, side):
-        if side == 0:
-            return pltpu.make_async_remote_copy(
-                src_ref=send_down.at[c, p], dst_ref=from_above.at[c, p], send_sem=edge_send.at[0, c, p],
-                recv_sem=edge_recv.at[0, c, p], device_id={"rb": b - 1}, device_id_type=MESH)
+    def outer_copy(c, p):
         return pltpu.make_async_remote_copy(
-            src_ref=send_up.at[c, p], dst_ref=from_below.at[c, p], send_sem=edge_send.at[1, c, p],
-            recv_sem=edge_recv.at[1, c, p], device_id={"rb": b + 1}, device_id_type=MESH)
+            src_ref=send_outer.at[c, p], dst_ref=arrived.at[jnp.where(odd, 0, 1), c, p],
+            send_sem=edge_send.at[0, c, p], recv_sem=edge_recv.at[0, c, p],
+            device_id={"rb": outer}, device_id_type=MESH)
+
+    def inner_copy(c, p):
+        return pltpu.make_async_remote_copy(
+            src_ref=send_inner.at[c, p], dst_ref=arrived.at[jnp.where(odd, 1, 0), c, p],
+            send_sem=edge_send.at[1, c, p], recv_sem=edge_recv.at[1, c, p],
+            device_id={"rb": inner_b}, device_id_type=MESH)
 
     dst_copy.start()
     psi_copy.start()
     src_copy.start()
     right_copy.start()
-    for p in range(2):
-        left_copy(0, p).start()
 
     barrier = pltpu.get_barrier_semaphore()
     for there, device in neighbours:
@@ -132,39 +140,42 @@
             pl.semaphore_signal(barrier, inc=1, device_id=device, device_id_type=MESH)
     @pl.when(b == 0)
     def _():
-        from_below[...] = jnp.zeros_like(from_below)
+        arrived[0] = jnp.zeros(arrived.shape[1:], BF)
 
     @pl.when(b == rb_size - 1)
     def _():
-        from_above[...] = jnp.zeros_like(from_above)
+        arrived[1] = jnp.zeros(arrived.shape[1:], BF)
 
     right_t[entries] = jnp.zeros((B, B), BF)
     for p in range(2):
         slots[p, groups] = jnp.zeros((B, 2 * B), F32)
 
     dst_copy.wait()
-    plan(terms, right_count, b * right_count, dst_ref, list_v, last_ref)
+    plan(terms, right_count, b * right_count, odd, dst_ref, list_v, last_ref)
     list_copy.start()
+    for p in range(2):
+        left_copy(0, p).start()
     psi_copy.wait()
 
     def turn_psi(s, carry):
-        for u in range(4):
-            at = pl.multiple_of((4 * s + u) * B, B)
-            psi_t[4 * s + u + SPAN] = out[pl.ds(at, B), :].T
+        for u in range(8):
+            at = pl.multiple_of((8 * s + u) * B, B)
+            psi_t[8 * s + u + SPAN] = out[pl.ds(at, B), :].T
         return carry
 
-    lax.fori_loop(0, left_count // 4, turn_psi, 0)
+    lax.fori_loop(0, left_count // 8, turn_psi, 0)
     right_copy.wait()
 
     def turn_right(w, carry):
-        for u in range(4):
+        for u in range(14):
             for j in range(right_count):
-                right_t[(4 * w + u) * right_count + j] = left_v[1, 4 * w + u, pl.ds(j * B, B), :].T
+                right_t[(14 * w + u) * right_count + j] = left_v[1, 14 * w + u, pl.ds(j * B, B), :].T
         return carry
 
-    lax.fori_loop(0, terms // 4, turn_right, 0)
+    lax.fori_loop(0, terms // 14, turn_right, 0)
 
     src_copy.wait()
+    list_copy.wait()
     pl.semaphore_wait(barrier, sum(there.astype(jnp.int32) for there, _ in neighbours))
 
     @pl.when(a > 0)
@@ -178,20 +189,18 @@
     zero = jnp.zeros((B, B), BF)
 
     def finish(c, p):
-        @pl.when(b > 0)
-        def _():
-            edge_copy(c, p, 1).wait_recv()
-
-        @pl.when(b < rb_size - 1)
-        def _():
-            edge_copy(c, p, 0).wait_recv()
+        inner_copy(c, p).wait_recv()
+
+        @pl.when(has_outer)
+        def _():
+            outer_copy(c, p).wait_recv()
 
         for j in range(right_count):
-            mine = slots[p, last_ref[SPAN + j]]
+            mine = slots[p, last_ref[jnp.where(odd, targets - 1 - SPAN - j, SPAN + j)]]
             if j < SPAN:
-                mine = mine + from_below[c, p, pl.ds(j * B, B), :].astype(F32)
+                mine = mine + arrived[0, c, p, pl.ds(j * B, B), :].astype(F32)
             if j >= right_count - SPAN:
-                mine = mine + from_above[c, p, pl.ds((j - right_count + SPAN) * B, B), :].astype(F32)
+                mine = mine + arrived[1, c, p, pl.ds((j - right_count + SPAN) * B, B), :].astype(F32)
             out[pl.ds(rows_of(c, p), 2 * B), pl.ds(j * B, B)] = mine.astype(BF).T
 
     def step(c, carry):
@@ -234,19 +243,11 @@
                 for j in range(right_count):
                     inner[w * right_count + j, :, pl.ds(p * 2 * B, 2 * B)] = y[j * B : (j + 1) * B]
 
-        @pl.when(c == 0)
-        def _():
-            list_copy.wait()
-
         def pair(n):
             return list_s[n // B, n % B]
 
-        for p in range(2):
-            @pl.when(c > 0)
-            def _():
-                finish(c - 1, p)
-
-            for g in range(groups):
+        def right_product(p, begin, end):
+            for g in range(begin, end):
                 at = [pair(GROUP * g + q) for q in range(GROUP)]
                 k = jnp.concatenate(
                     [inner[jnp.clip(e, 0, entries - 1), :, pl.ds(p * 2 * B, 2 * B)] for e in at], axis=0)
@@ -255,18 +256,43 @@
                 if g > 0:
                     y = y + jnp.where(pair(LISTED + g) == 1, slots[p, g - 1], 0.0)
                 slots[p, g] = y
+
+        def before(p):
+            @pl.when(c > 0)
+            def _():
+                finish(c - 1, p)
+
+        def to_outer(p):
             for k in range(SPAN):
-                send_down[c, p, pl.ds(k * B, B), :] = slots[p, last_ref[k]].astype(BF)
-                send_up[c, p, pl.ds(k * B, B), :] = slots[p, last_ref[SPAN + right_count + k]].astype(BF)
-
-            @pl.when(b > 0)
-            def _():
-                edge_copy(c, p, 0).start()
-
-            @pl.when(b < rb_size - 1)
-            def _():
-                edge_copy(c, p, 1).start()
-
+                send_outer[c, p, pl.ds(k * B, B), :] = slots[p, last_ref[jnp.where(odd, SPAN - 1 - k, k)]].astype(BF)
+
+            @pl.when(has_outer)
+            def _():
+                outer_copy(c, p).start()
+
+        def to_inner(p):
+            for k in range(SPAN):
+                at = last_ref[jnp.where(odd, targets - 1 - k, targets - SPAN + k)]
+                send_inner[c, p, pl.ds(k * B, B), :] = slots[p, at].astype(BF)
+            inner_copy(c, p).start()
+
+        @pl.when(c < chunks - 1)
+        def _():
+            for p in range(2):
+                before(p)
+                right_product(p, 0, groups)
+                to_outer(p)
+                to_inner(p)
+
+        @pl.when(c == chunks - 1)
+        def _():
+            for p in range(2):
+                before(p)
+                right_product(p, 0, early)
+                to_outer(p)
+            for p in range(2):
+                right_product(p, early, groups)
+                to_inner(p)
         return carry
 
     lax.fori_loop(0, chunks, step, 0)
@@ -275,13 +301,11 @@
 
     def drain(c, carry):
         for p in range(2):
-            @pl.when(b > 0)
-            def _():
-                edge_copy(c, p, 0).wait_send()
-
-            @pl.when(b < rb_size - 1)
-            def _():
-                edge_copy(c, p, 1).wait_send()
+            inner_copy(c, p).wait_send()
+
+            @pl.when(has_outer)
+            def _():
+                outer_copy(c, p).wait_send()
         return carry
 
     lax.fori_loop(0, chunks, drain, 0)
@@ -323,7 +347,7 @@
             pltpu.VMEM((2, terms, width, B), BF),
             pltpu.VMEM((entries, B, width), BF),
             pltpu.VMEM((2, groups + 1, B, 2 * B), F32),
-            edge, edge, edge, edge,
+            edge, edge, pltpu.VMEM((2, chunks, 2, halo, 2 * B), BF),
             dma((2,)), dma(()), dma(()), dma(()), dma((2, 2)), dma((2,)), dma((2,)), dma((2, chunks, 2)), dma((2, chunks, 2)),
         ],
         compiler_params=pltpu.CompilerParams(

time: 43.8 us -> 42.7 us (0.975)
  Pallas kernels: 42.3 us -> 41.2 us
    pallas_call x1, Pallas kernels: 42.3 us -> 41.2 us  [on_device(): pl.pallas_call(functools.partial(main_kernel, (lb_size, rb_size, terms, l...]
where the time goes in v4:
time: 42.7 us; the launch traced here: 42.6 us
  Pallas kernels  41.2 us (96%)
  local copies, waits for them, and re-layouts  1.32 us (3%)
    pallas_call x1, Pallas kernels, on_device(): pl.pallas_call(functools.partial(main_kernel, (lb_size, rb_size, terms, l...  41.2 us
    unnamed x1, local copies, waits for them, and re-layouts  1.32 us

profile of v4, /device:TPU:25, one launch (start us, length us, event | category | flops | bytes accessed | tf_op | source)
XLA Modules:
  0.0 42.6 jit_solution(11627821584216529193)
XLA Ops:
  0.0 41.2 %apply.1 = bf16[2048,512]{1,0:T(8,128)(2,1)S(1)} custom-call(s32[28,128]{1,0:T(8,128)} %src.1, s32[28,64]{1,0:T(8,128)} %dst.1, bf16[2048,512]{1,0:T(8,128)(2,1)} %psi.1, bf16[28,2048,128]{2,1,0:T(8,128)(2,1)} %left.1, bf16[28,512,128]{2,1,0:T(8,128)(2,1)} %right.1), custom_call_target="tpu_custom_call" | custom-call | tf_op jit(solution)/shard_map/apply/pallas_call | solution.py:332
  41.2 1.3 %copy.7 = bf16[2048,512]{1,0:T(8,128)(2,1)} copy(bf16[2048,512]{1,0:T(8,128)(2,1)S(1)} %apply.1) | data formatting | bytes 4194304

commit v5 on v4

--- a/solution.py
+++ b/solution.py
@@ -262,37 +262,41 @@
             def _():
                 finish(c - 1, p)
 
-        def to_outer(p):
+        def fill_outer(p):
             for k in range(SPAN):
                 send_outer[c, p, pl.ds(k * B, B), :] = slots[p, last_ref[jnp.where(odd, SPAN - 1 - k, k)]].astype(BF)
 
+        def start_outer(p):
             @pl.when(has_outer)
             def _():
                 outer_copy(c, p).start()
 
-        def to_inner(p):
+        def fill_inner(p):
             for k in range(SPAN):
                 at = last_ref[jnp.where(odd, targets - 1 - k, targets - SPAN + k)]
                 send_inner[c, p, pl.ds(k * B, B), :] = slots[p, at].astype(BF)
-            inner_copy(c, p).start()
 
         @pl.when(c < chunks - 1)
         def _():
             for p in range(2):
                 before(p)
                 right_product(p, 0, groups)
-                to_outer(p)
-                to_inner(p)
+                fill_outer(p)
+                fill_inner(p)
+                inner_copy(c, p).start()
+                start_outer(p)
 
         @pl.when(c == chunks - 1)
         def _():
             for p in range(2):
                 before(p)
                 right_product(p, 0, early)
-                to_outer(p)
+                fill_outer(p)
+                start_outer(p)
             for p in range(2):
                 right_product(p, early, groups)
-                to_inner(p)
+                fill_inner(p)
+                inner_copy(c, p).start()
         return carry
 
     lax.fori_loop(0, chunks, step, 0)

time: 42.7 us -> 42.7 us (level)
  no operation moved by 1% of the time
where the time goes in v5:
time: 42.7 us; the launch traced here: 42.5 us
  Pallas kernels  41.2 us (96%)
  local copies, waits for them, and re-layouts  1.32 us (3%)
    pallas_call x1, Pallas kernels, on_device(): pl.pallas_call(functools.partial(main_kernel, (lb_size, rb_size, terms, l...  41.2 us
    unnamed x1, local copies, waits for them, and re-layouts  1.32 us

profile of v5, /device:TPU:25, one launch (start us, length us, event | category | flops | bytes accessed | tf_op | source)
XLA Modules:
  0.0 42.5 jit_solution(7563687158012003345)
XLA Ops:
  0.0 41.2 %apply.1 = bf16[2048,512]{1,0:T(8,128)(2,1)S(1)} custom-call(s32[28,128]{1,0:T(8,128)} %src.1, s32[28,64]{1,0:T(8,128)} %dst.1, bf16[2048,512]{1,0:T(8,128)(2,1)} %psi.1, bf16[28,2048,128]{2,1,0:T(8,128)(2,1)} %left.1, bf16[28,512,128]{2,1,0:T(8,128)(2,1)} %right.1), custom_call_target="tpu_custom_call" | custom-call | tf_op jit(solution)/shard_map/apply/pallas_call | solution.py:336
  41.2 1.3 %copy.7 = bf16[2048,512]{1,0:T(8,128)(2,1)} copy(bf16[2048,512]{1,0:T(8,128)(2,1)S(1)} %apply.1) | data formatting | bytes 4194304
